TPU v7x, 128 devices: a whole 4x4x4 slice. The times are simulated.
128 devices in a mesh: expert: 4 (over y), feat: 32 (over x, z, core).
Axes of the slice: x: 4, y: 4, z: 4, core: 2. Of those that a mesh axis runs over, the one named last changes fastest.
Arguments:
- tokens: bfloat16 [1024, 4096], P(('expert', 'feat')), may hold values from -6 to 6
- expert_ids: int32 [1024, 2], P(('expert', 'feat')), may hold values from 0 to 7, as said below
- route_weights: bfloat16 [1024, 2], P(('expert', 'feat')), may hold values from 0.099609375 to 1
- gate_proj: bfloat16 [4096, 28672], P(None, ('expert', 'feat')), may hold values from -0.09375 to 0.09375
- up_proj: bfloat16 [4096, 28672], P(None, ('expert', 'feat')), may hold values from -0.09375 to 0.09375
- down_proj: bfloat16 [28672, 4096], P(('expert', 'feat')), may hold values from -0.046875 to 0.046875
- enc_weight: float32 [4096, 32768], P(None, ('expert', 'feat')), may hold values from -0.09375 to 0.09375
- enc_bias: float32 [32768], P(('expert', 'feat')), may hold values from -3 to 3
- log_threshold: float32 [32768], P(('expert', 'feat')), may hold values from -2.3 to 0
- dec_weight: float32 [32768, 4096], P(('expert', 'feat')), may hold values from -0.046875 to 0.046875
Outputs:
- grad_encoder: float32 [4096, 32768], P(None, ('expert', 'feat'))
- grad_decoder: float32 [32768, 4096], P(('expert', 'feat'))
- grad_bias: float32 [32768], P(('expert', 'feat'))
- grad_threshold: float32 [32768], P(('expert', 'feat'))
Inputs may be any that keep to these rules, and one draw needn't show every extreme that they name: `expert_ids`: each token names two different experts of 0 to 7. Among the 8 tokens of one device, each expert below 2 is named by at most 4 tokens; in every draw one of these experts, drawn from the seed and the same for all devices, is named by exactly 4 tokens of every device.
All inputs are finite; a program needn't handle non-finite values.
Results may differ from a plain program's by a relative error of at most 0.0021.
Values may be sent and summed in bfloat16 or wider, within the bound.
A program may use at most 128 MiB of HBM per device.

v0:
```python
import jax
import jax.numpy as jnp
from jax import lax
from jax.sharding import PartitionSpec as P

sharpness = 0.1
kernel_width = 0.5
density_weight = 0.01
highest = lax.Precision.HIGHEST


def partner(block, axis, stride):
    count = lax.axis_size(axis)
    route = []
    for low in range(count):
        high = low | 1 << stride
        if high != low and high < count:
            route += [(low, high), (high, low)]
    return lax.ppermute(block, axis, route)


def pack_slots(tokens, expert_ids, route_weights, experts):
    capacity = tokens.shape[0] // 2
    window = jnp.arange(experts, dtype=jnp.int32)
    matches = expert_ids[:, :, None] == window[None, None, :]
    named = jnp.sum(matches.astype(jnp.int32), axis=1)
    weighted = jnp.sum(
        jnp.where(matches, route_weights[:, :, None], jnp.zeros((), jnp.bfloat16)), axis=1
    )
    slot_index = jnp.cumsum(named, axis=0) - named
    places = jnp.arange(capacity, dtype=jnp.int32)
    chosen = (named.T[:, None, :] == 1) & (slot_index.T[:, None, :] == places[None, :, None])
    slot_rows = jnp.einsum(
        "ect,td->ecd", chosen.astype(jnp.bfloat16), tokens, preferred_element_type=jnp.float32
    ).astype(jnp.bfloat16)
    slot_weights = jnp.sum(
        jnp.where(chosen, weighted.T[:, None, :], jnp.zeros((), jnp.bfloat16)), axis=2
    )
    return (slot_rows, slot_weights)


def contract_rows(left, right):
    return lax.dot_general(left, right, (((0,), (0,)), ((), ())), precision=highest)


def body(
    tokens,
    expert_ids,
    route_weights,
    gate_proj,
    up_proj,
    down_proj,
    enc_weight,
    enc_bias,
    log_threshold,
    dec_weight,
):
    copies = 2
    experts = lax.axis_size("expert") // copies
    slot_rows, slot_weights = pack_slots(tokens, expert_ids, route_weights, experts)
    send_rows = jnp.repeat(slot_rows, copies, axis=0)
    send_weights = jnp.repeat(slot_weights, copies, axis=0)
    came_rows, came_weights = (
        lax.all_to_all(send_rows, "expert", split_axis=0, concat_axis=0, tiled=True),
        lax.all_to_all(send_weights, "expert", split_axis=0, concat_axis=0, tiled=True),
    )
    all_rows, all_weights = (
        lax.all_gather(came_rows, "feat", axis=0, tiled=True),
        lax.all_gather(came_weights, "feat", axis=0, tiled=True),
    )
    width = tokens.shape[1]
    token_rows = all_rows.reshape(-1, width)
    row_weights = all_weights.reshape(-1).astype(jnp.float32)
    gate_act = jnp.dot(token_rows, gate_proj, preferred_element_type=jnp.float32)
    up_act = jnp.dot(token_rows, up_proj, preferred_element_type=jnp.float32)
    hidden = (jax.nn.silu(gate_act) * up_act).astype(jnp.bfloat16)
    target_part = jnp.dot(hidden, down_proj, preferred_element_type=jnp.float32)
    inputs = token_rows.astype(jnp.float32)
    preact = jnp.dot(inputs, enc_weight, precision=highest) + enc_bias
    threshold = jnp.exp(log_threshold)
    shifted = preact - threshold
    soft_gate = jax.nn.sigmoid(shifted / sharpness)
    active = preact * soft_gate
    partial_error = jnp.dot(active, dec_weight, precision=highest) - target_part
    feat_total = lax.psum(partial_error, "feat")
    recon_error = feat_total + partner(feat_total, "expert", 0)
    residual_grad = 2.0 * row_weights[:, None] * recon_error
    grad_decoder = contract_rows(active, residual_grad)
    grad_active = lax.dot_general(
        residual_grad, dec_weight, (((1,), (1,)), ((), ())), precision=highest
    )
    grad_pre = grad_active * soft_gate
    grad_encoder = contract_rows(inputs, grad_pre)
    grad_bias = jnp.sum(grad_pre, axis=0)
    kernel = jnp.maximum(0.0, 1.0 - jnp.abs(shifted) / kernel_width) / kernel_width
    slope_sum = jnp.sum(
        (grad_active * threshold + density_weight * row_weights[:, None]) * kernel, axis=0
    )
    grad_threshold = -threshold * slope_sum
    return (grad_encoder, grad_decoder, grad_bias, grad_threshold)


def solution(mesh):
    in_specs = (
        P(("expert", "feat"), None),
        P(("expert", "feat"), None),
        P(("expert", "feat"), None),
        P(None, ("expert", "feat")),
        P(None, ("expert", "feat")),
        P(("expert", "feat"), None),
        P(None, ("expert", "feat")),
        P(("expert", "feat")),
        P(("expert", "feat")),
        P(("expert", "feat"), None),
    )
    out_specs = (
        P(None, ("expert", "feat")),
        P(("expert", "feat"), None),
        P(("expert", "feat")),
        P(("expert", "feat")),
    )
    return jax.shard_map(body, mesh=mesh, in_specs=in_specs, out_specs=out_specs, check_vma=False)
```

profile of v0, /device:TPU:1, one launch (start us, length us, event | category | flops | bytes accessed | tf_op | source)
XLA Modules:
  0.0 474.6 jit_solution(3377354966974964132)
XLA Ops:
  7.2 0.8 convert_reduce_fusion
  8.1 0.2 reduce_window_sum.11
  8.2 1.0 convolution_convert_fusion
  9.3 9.7 %all_to_all.17 = bf16[4,4,4096]{2,1,0:T(4,128)(2,1)} all-to-all(bf16[4,4,4096]{2,1,0:T(4,128)(2,1)S(1)} %bitcast.20), channel_id=1, replica_groups=mesh['expert'=4,'feat'=32] {'expert'}, dimensions={0} | all-to-all | bytes 262144 | tf_op jit(solution)/shard_map/all_to_all | solution.py:64
  19.0 0.0 all-reduce.2.cloned.1.call-start
  19.1 0.7 exp.10
  19.8 48.0 %all-gather.3.cloned.1.call-done = bf16[128,4,4096]{2,1,0:T(4,128)(2,1)} async-done(((bf16[4,4,4096]{2,1,0:T(4,128)(2,1)}), bf16[128,4,4096]{2,1,0:T(4,128)(2,1)}) %all-gather.3.cloned.1.call-update) | async-done | bytes 4194320 | tf_op jit(solution)/shard_map/all_gather | solution.py:68
  67.8 6.9 %reshape.45 = bf16[512,4096]{1,0:T(8,128)(2,1)} reshape(bf16[128,4,4096]{2,1,0:T(4,128)(2,1)} %all-gather.3.cloned.1.call-done) | data formatting | bytes 8388608 | tf_op jit(solution)/shard_map/reshape | solution.py:72
  74.7 4.3 fusion.31
  79.0 5.8 %convolution_add_fusion = f32[512,256]{1,0:T(8,128)S(1)} fusion(bf16[512,4096]{1,0:T(8,128)(2,1)S(1)} %copy-done.1, f32[4096,256]{1,0:T(8,128)} %param.16, f32[256]{0:T(256)S(1)} %copy-done.7), kind=kOutput, calls=%fused_computation.6 | convolution fusion | flops 6442582016 | bytes 8913920 | tf_op jit(solution)/shard_map/dot_general | solution.py:79
  84.9 8.7 %fusion.3 = f32[512,4096]{1,0:T(8,128)} fusion(bf16[224,4096]{1,0:T(8,128)(2,1)S(1)} %copy-done, bf16[512,4096]{1,0:T(8,128)(2,1)} %reshape.45, bf16[4096,224]{0,1:T(8,128)(2,1)} %param.14, f32[512,224]{0,1:T(8,128)S(1)} %fusion.31), kind=kOutput, calls=%fused_computation.8 | convolution fusion | flops 1879736320 | bytes 16711680 | tf_op jit(solution)/shard_map/dot_general | solution.py:77
  93.6 13.0 %convolution_subtract_fusion = f32[512,4096]{1,0:T(8,128)} fusion(f32[512,4096]{1,0:T(8,128)} %fusion.3, f32[256,4096]{1,0:T(8,128)} %param.19, f32[512,256]{1,0:T(8,128)S(1)} %convolution_add_fusion, f32[256]{0:T(256)S(1)} %exp.10), kind=kOutput, calls=%fused_computation.1 | convolution fusion | flops 6445334528 | bytes 21496832 | tf_op jit(solution)/shard_map/dot_general | solution.py:84
  106.6 119.7 %all-reduce.2.cloned.1.call-done = f32[512,4096]{1,0:T(8,128)} async-done(((f32[512,4096]{1,0:T(8,128)}), f32[512,4096]{1,0:T(8,128)}) %all-reduce.2.cloned.1.call-update) | async-done | bytes 8388624 | tf_op jit(solution)/shard_map/psum | solution.py:85
  226.4 1.2 collective-permute-start
  227.6 0.1 fusion.18
  227.7 181.8 %all_to_all.18 = bf16[4,1,4]{2,1,0:T(2,128)(2,1)S(1)} all-to-all(bf16[4,1,4]{2,1,0:T(2,128)(2,1)S(1)} %copy.21), channel_id=1, replica_groups=mesh['expert'=4,'feat'=32] {'expert'}, dimensions={0} | all-to-all | bytes 64 | tf_op jit(solution)/shard_map/all_to_all | solution.py:65
  409.5 26.1 %all-gather = bf16[128,1,4]{2,1,0:T(2,128)(2,1)S(1)} all-gather(bf16[4,1,4]{2,1,0:T(2,128)(2,1)S(1)} %all_to_all.18), channel_id=2, replica_groups=mesh['expert'=4,'feat'=32] {'feat'}, dimensions={0}, use_global_device_ids=true | all-gather | bytes 1056 | tf_op jit(solution)/shard_map/all_gather | solution.py:69
  435.6 0.4 multiply_reduce_fusion.1
  436.0 0.1 mul.73
  436.1 0.1 mul.63
  436.2 13.2 %multiply_reduce_fusion = (f32[256]{0:T(256)S(1)}, f32[256]{0:T(256)}, f32[512,256]{1,0:T(8,128)S(1)}) fusion(f32[512,256]{1,0:T(8,128)S(1)} %convolution_add_fusion, f32[512]{0:T(512)S(1)} %mul.73, f32[256]{0:T(256)S(1)} %exp.10, f32[256,4096]{1,0:T(8,128)} %param.19, f32[512,4096]{1,0:T(8,128)} %all-reduce.2.cloned.1.call-done, ...), kind=kOutput, calls=%fused_computation.9 | convolution fusion | flops 6448741888 | bytes 22027264 | tf_op jit(solution)/shard_map/dot_general | solution.py:89
  449.4 6.3 %fusion.29 = f32[4096,256]{1,0:T(8,128)} fusion(bf16[512,4096]{1,0:T(8,128)(2,1)S(1)} %copy-done.2, f32[512,256]{1,0:T(8,128)S(1)} %get-tuple-element.8, f32[512,256]{1,0:T(8,128)S(1)} %convolution_add_fusion, f32[256]{0:T(256)S(1)} %exp.10), kind=kOutput, calls=%fused_computation.41 | convolution fusion | flops 6443237376 | bytes 9438208 | tf_op jit(solution)/shard_map/dot_general | solution.py:43
  455.7 0.6 negate_multiply_fusion
  456.3 11.5 %fusion = f32[256,4096]{1,0:T(8,128)} fusion(f32[512,4096]{1,0:T(8,128)S(1)} %copy-done.3, f32[512,4096]{1,0:T(8,128)} %collective-permute-done, f32[512]{0:T(512)S(1)} %mul.63, f32[512,256]{1,0:T(8,128)S(1)} %convolution_add_fusion, f32[256]{0:T(256)S(1)} %exp.10), kind=kOutput, calls=%fused_computation.4 | convolution fusion | flops 6447431680 | bytes 21498880 | tf_op jit(solution)/shard_map/dot_general | solution.py:43
  (26 shorter events, 0.2 us)
Async XLA Ops:
  7.2 77.7 %copy-start = (bf16[224,4096]{1,0:T(8,128)(2,1)S(1)}, bf16[224,4096]{1,0:T(8,128)(2,1)}, u32[]{:S(2)}) copy-start(bf16[224,4096]{1,0:T(8,128)(2,1)} %param.15) | copy-start | bytes 5505028
  7.2 60.6 %all-gather.3.cloned.1.call-start = ((), (), s32[]{:S(2)}) async-start(), calls=%async_computation.2 | async-start | bytes 4325376 | tf_op jit(solution)/shard_map/all_gather | solution.py:68
  19.0 207.3 %all-reduce.2.cloned.1.call-start = ((), (), s32[]{:S(2)}) async-start(), calls=%async_computation.3 | async-start | bytes 16777216 | tf_op jit(solution)/shard_map/psum | solution.py:85
  74.7 4.4 copy-start.1
  74.7 4.4 copy-start.7
  106.6 121.0 %copy-start.5 = (s32[8,2]{0,1:T(2,128)S(1)}, s32[8,2]{0,1:T(2,128)}, u32[]{:S(2)}) copy-start(s32[8,2]{0,1:T(2,128)} %param.11) | copy-start | bytes 196
  106.6 121.0 %copy-start.6 = (bf16[8,2]{0,1:T(2,128)(2,1)S(1)}, bf16[8,2]{0,1:T(2,128)(2,1)}, u32[]{:S(2)}) copy-start(bf16[8,2]{0,1:T(2,128)(2,1)} %param.12) | copy-start | bytes 100
  226.4 209.8 %collective-permute-start = (f32[512,4096]{1,0:T(8,128)}, f32[512,4096]{1,0:T(8,128)}, u32[]{:S(2)}, u32[]{:S(2)}) collective-permute-start(f32[512,4096]{1,0:T(8,128)} %all-reduce.2.cloned.1.call-done), channel_id=1, source_target_pairs={{0,32},{32,0},{64,96},{96,64},{1,33},{33,1},{65,97},{97,65},{2,34}... | collective-permute-start | bytes 25165832 | tf_op jit(solution)/shard_map/ppermute | solution.py:19
  436.2 13.2 %copy-start.2 = (bf16[512,4096]{1,0:T(8,128)(2,1)S(1)}, bf16[512,4096]{1,0:T(8,128)(2,1)}, u32[]{:S(2)}) copy-start(bf16[512,4096]{1,0:T(8,128)(2,1)} %reshape.45) | copy-start | bytes 12582916
  449.4 6.3 %copy-start.4 = (f32[256]{0:T(256)S(1)}, f32[256]{0:T(256)}, u32[]{:S(2)}) copy-start(f32[256]{0:T(256)} %param.18) | copy-start | bytes 3076
  449.4 6.9 %copy-start.3 = (f32[512,4096]{1,0:T(8,128)S(1)}, f32[512,4096]{1,0:T(8,128)}, u32[]{:S(2)}) copy-start(f32[512,4096]{1,0:T(8,128)} %all-reduce.2.cloned.1.call-done) | copy-start | bytes 25165828
Sparse Core Ops, SparseCore 0:
  19.2 48.5 all-gather.2
  106.8 119.5 all-reduce.1
where the time goes:
time: 475 us
  blocking collectives  218 us (46%)
  waiting for transfers between devices  168 us (35%)
  matrix products  63.9 us (13%)
  between operations  14.1 us (3%)
  local copies, waits for them, and re-layouts  7.86 us (2%)
    all_to_all x1, blocking collectives, body(): lax.all_to_all(send_weights, 'expert', split_axis=0, concat_axis=0, tiled...  182 us
    psum x1, waiting for transfers between devices, body(): feat_total = lax.psum(partial_error, 'feat')  120 us
    all_gather x1, waiting for transfers between devices, body(): lax.all_gather(came_rows, 'feat', axis=0, tiled=True)  48 us
    all_gather x1, blocking collectives, body(): lax.all_gather(came_weights, 'feat', axis=0, tiled=True)  26.1 us
    dot_general x2, matrix products, contract_rows(): lax.dot_general(left, right, (((0,), (0,)), ((), ())), precision=highest)  17.8 us
    dot_general x1, matrix products, body(): lax.dot_general(residual_grad, dec_weight, (((1,), (1,)), ((), ())), prec...  13.2 us
    dot_general x1, matrix products, body(): partial_error = jnp.dot(active, dec_weight, precision=highest) - target_part  13 us
    all_to_all x1, blocking collectives, body(): lax.all_to_all(send_rows, 'expert', split_axis=0, concat_axis=0, tiled=True)  9.75 us
  transfers between devices with their start and end apart: 3, of which 2 were waited for; matrix products, arithmetic and copies ran while one was open for 0% of the time, Pallas kernels for 0%

commit v1 on v0

--- a/solution.py
+++ b/solution.py
@@ -66,7 +66,9 @@
     )
     all_rows, all_weights = (
         lax.all_gather(came_rows, "feat", axis=0, tiled=True),
-        lax.all_gather(came_weights, "feat", axis=0, tiled=True),
+        jnp.concatenate(
+            lax.all_to_all(jnp.stack([came_weights] * lax.axis_size("feat")), "feat", 0, 0), axis=0
+        ),
     )
     width = tokens.shape[1]
     token_rows = all_rows.reshape(-1, width)

time: 475 us -> 463 us (0.975)
  blocking collectives: 218 us -> 206 us
    all_gather x1 -> x0, blocking collectives: 26.1 us -> none  [body(): lax.all_gather(came_weights, 'feat', axis=0, tiled=True)]
    all_to_all x0 -> x1, blocking collectives: none -> 14.5 us  [body(): lax.all_to_all(jnp.stack([came_weights] * lax.axis_size('feat')), 'feat',...]
where the time goes in v1:
time: 463 us
  blocking collectives  206 us (44%)
  waiting for transfers between devices  168 us (36%)
  matrix products  63.9 us (14%)
  between operations  14.1 us (3%)
  local copies, waits for them, and re-layouts  7.9 us (2%)
    all_to_all x1, blocking collectives, body(): lax.all_to_all(send_weights, 'expert', split_axis=0, concat_axis=0, tiled...  182 us
    psum x1, waiting for transfers between devices, body(): feat_total = lax.psum(partial_error, 'feat')  120 us
    all_gather x1, waiting for transfers between devices, body(): lax.all_gather(came_rows, 'feat', axis=0, tiled=True)  48 us
    dot_general x2, matrix products, contract_rows(): lax.dot_general(left, right, (((0,), (0,)), ((), ())), precision=highest)  17.8 us
    all_to_all x1, blocking collectives, body(): lax.all_to_all(jnp.stack([came_weights] * lax.axis_size('feat')), 'feat',...  14.5 us
    dot_general x1, matrix products, body(): lax.dot_general(residual_grad, dec_weight, (((1,), (1,)), ((), ())), prec...  13.2 us
    dot_general x1, matrix products, body(): partial_error = jnp.dot(active, dec_weight, precision=highest) - target_part  13 us
    all_to_all x1, blocking collectives, body(): lax.all_to_all(send_rows, 'expert', split_axis=0, concat_axis=0, tiled=True)  9.75 us
  transfers between devices with their start and end apart: 3, of which 2 were waited for; matrix products, arithmetic and copies ran while one was open for 0% of the time, Pallas kernels for 0%

profile of v1, /device:TPU:1, one launch (start us, length us, event | category | flops | bytes accessed | tf_op | source)
XLA Modules:
  0.0 462.7 jit_solution(16110298809443467607)
XLA Ops:
  7.2 0.0 all-gather.2.cloned.1.call-start
  7.2 0.8 convert_reduce_fusion
  8.1 0.2 reduce_window_sum.11
  8.2 1.0 convolution_convert_fusion
  9.3 9.7 %all_to_all.19 = bf16[4,4,4096]{2,1,0:T(4,128)(2,1)} all-to-all(bf16[4,4,4096]{2,1,0:T(4,128)(2,1)S(1)} %bitcast.23), channel_id=1, replica_groups=mesh['expert'=4,'feat'=32] {'expert'}, dimensions={0} | all-to-all | bytes 262144 | tf_op jit(solution)/shard_map/all_to_all | solution.py:64
  19.0 0.0 all-reduce.2.cloned.1.call-start
  19.1 0.7 exp.10
  19.8 48.0 %all-gather.2.cloned.1.call-done = bf16[128,4,4096]{2,1,0:T(4,128)(2,1)} async-done(((bf16[4,4,4096]{2,1,0:T(4,128)(2,1)}), bf16[128,4,4096]{2,1,0:T(4,128)(2,1)}) %all-gather.2.cloned.1.call-update) | async-done | bytes 4194320 | tf_op jit(solution)/shard_map/all_gather | solution.py:68
  67.8 6.9 %reshape.47 = bf16[512,4096]{1,0:T(8,128)(2,1)} reshape(bf16[128,4,4096]{2,1,0:T(4,128)(2,1)} %all-gather.2.cloned.1.call-done) | data formatting | bytes 8388608 | tf_op jit(solution)/shard_map/reshape | solution.py:74
  74.7 4.3 fusion.31
  79.0 5.8 %convolution_add_fusion = f32[512,256]{1,0:T(8,128)S(1)} fusion(bf16[512,4096]{1,0:T(8,128)(2,1)S(1)} %copy-done.1, f32[4096,256]{1,0:T(8,128)} %param.16, f32[256]{0:T(256)S(1)} %copy-done.7), kind=kOutput, calls=%fused_computation.6 | convolution fusion | flops 6442582016 | bytes 8913920 | tf_op jit(solution)/shard_map/dot_general | solution.py:81
  84.9 8.7 %fusion.3 = f32[512,4096]{1,0:T(8,128)} fusion(bf16[224,4096]{1,0:T(8,128)(2,1)S(1)} %copy-done, bf16[512,4096]{1,0:T(8,128)(2,1)} %reshape.47, bf16[4096,224]{0,1:T(8,128)(2,1)} %param.14, f32[512,224]{0,1:T(8,128)S(1)} %fusion.31), kind=kOutput, calls=%fused_computation.8 | convolution fusion | flops 1879736320 | bytes 16711680 | tf_op jit(solution)/shard_map/dot_general | solution.py:79
  93.6 13.0 %convolution_subtract_fusion = f32[512,4096]{1,0:T(8,128)} fusion(f32[512,4096]{1,0:T(8,128)} %fusion.3, f32[256,4096]{1,0:T(8,128)} %param.19, f32[512,256]{1,0:T(8,128)S(1)} %convolution_add_fusion, f32[256]{0:T(256)S(1)} %exp.10), kind=kOutput, calls=%fused_computation.1 | convolution fusion | flops 6445334528 | bytes 21496832 | tf_op jit(solution)/shard_map/dot_general | solution.py:86
  106.6 119.7 %all-reduce.2.cloned.1.call-done = f32[512,4096]{1,0:T(8,128)} async-done(((f32[512,4096]{1,0:T(8,128)}), f32[512,4096]{1,0:T(8,128)}) %all-reduce.2.cloned.1.call-update) | async-done | bytes 8388624 | tf_op jit(solution)/shard_map/psum | solution.py:87
  226.4 1.2 collective-permute-start
  227.6 0.1 fusion.18
  227.7 181.8 %all_to_all.20 = bf16[4,1,4]{2,1,0:T(2,128)(2,1)S(1)} all-to-all(bf16[4,1,4]{2,1,0:T(2,128)(2,1)S(1)} %copy.24), channel_id=1, replica_groups=mesh['expert'=4,'feat'=32] {'expert'}, dimensions={0} | all-to-all | bytes 64 | tf_op jit(solution)/shard_map/all_to_all | solution.py:65
  409.5 14.5 %all_to_all.21 = bf16[32,4,4]{2,1,0:T(4,128)(2,1)S(1)} all-to-all(bf16[32,4,4]{2,1,0:T(4,128)(2,1)S(1)} %stack.5), channel_id=1, replica_groups=mesh['expert'=4,'feat'=32] {'feat'}, dimensions={0} | all-to-all | bytes 2048 | tf_op jit(solution)/shard_map/all_to_all | solution.py:70
  424.1 0.1 mul.73
  424.2 0.1 mul.63
  424.3 13.2 %multiply_reduce_fusion = (f32[256]{0:T(256)S(1)}, f32[256]{0:T(256)}, f32[512,256]{1,0:T(8,128)S(1)}) fusion(f32[512,256]{1,0:T(8,128)S(1)} %convolution_add_fusion, f32[512]{0:T(512)S(1)} %mul.73, f32[256]{0:T(256)S(1)} %exp.10, f32[256,4096]{1,0:T(8,128)} %param.19, f32[512,4096]{1,0:T(8,128)} %all-reduce.2.cloned.1.call-done, ...), kind=kOutput, calls=%fused_computation.9 | convolution fusion | flops 6448741888 | bytes 22027264 | tf_op jit(solution)/shard_map/dot_general | solution.py:91
  437.5 6.3 %fusion.29 = f32[4096,256]{1,0:T(8,128)} fusion(bf16[512,4096]{1,0:T(8,128)(2,1)S(1)} %copy-done.2, f32[512,256]{1,0:T(8,128)S(1)} %get-tuple-element.8, f32[512,256]{1,0:T(8,128)S(1)} %convolution_add_fusion, f32[256]{0:T(256)S(1)} %exp.10), kind=kOutput, calls=%fused_computation.42 | convolution fusion | flops 6443237376 | bytes 9438208 | tf_op jit(solution)/shard_map/dot_general | solution.py:43
  443.8 0.6 negate_multiply_fusion
  444.4 11.5 %fusion = f32[256,4096]{1,0:T(8,128)} fusion(f32[512,4096]{1,0:T(8,128)S(1)} %copy-done.3, f32[512,4096]{1,0:T(8,128)} %collective-permute-done, f32[512]{0:T(512)S(1)} %mul.63, f32[512,256]{1,0:T(8,128)S(1)} %convolution_add_fusion, f32[256]{0:T(256)S(1)} %exp.10), kind=kOutput, calls=%fused_computation.4 | convolution fusion | flops 6447431680 | bytes 21498880 | tf_op jit(solution)/shard_map/dot_general | solution.py:43
  (28 shorter events, 0.2 us)
Async XLA Ops:
  7.2 77.7 %copy-start = (bf16[224,4096]{1,0:T(8,128)(2,1)S(1)}, bf16[224,4096]{1,0:T(8,128)(2,1)}, u32[]{:S(2)}) copy-start(bf16[224,4096]{1,0:T(8,128)(2,1)} %param.15) | copy-start | bytes 5505028
  7.2 60.6 %all-gather.2.cloned.1.call-start = ((), (), s32[]{:S(2)}) async-start(), calls=%async_computation.3 | async-start | bytes 4325376 | tf_op jit(solution)/shard_map/all_gather | solution.py:68
  19.0 207.3 %all-reduce.2.cloned.1.call-start = ((), (), s32[]{:S(2)}) async-start(), calls=%async_computation.4 | async-start | bytes 16777216 | tf_op jit(solution)/shard_map/psum | solution.py:87
  74.7 4.4 copy-start.1
  74.7 4.4 copy-start.7
  106.6 121.0 %copy-start.5 = (s32[8,2]{0,1:T(2,128)S(1)}, s32[8,2]{0,1:T(2,128)}, u32[]{:S(2)}) copy-start(s32[8,2]{0,1:T(2,128)} %param.11) | copy-start | bytes 196
  106.6 121.0 %copy-start.6 = (bf16[8,2]{0,1:T(2,128)(2,1)S(1)}, bf16[8,2]{0,1:T(2,128)(2,1)}, u32[]{:S(2)}) copy-start(bf16[8,2]{0,1:T(2,128)(2,1)} %param.12) | copy-start | bytes 100
  226.4 197.9 %collective-permute-start = (f32[512,4096]{1,0:T(8,128)}, f32[512,4096]{1,0:T(8,128)}, u32[]{:S(2)}, u32[]{:S(2)}) collective-permute-start(f32[512,4096]{1,0:T(8,128)} %all-reduce.2.cloned.1.call-done), channel_id=1, source_target_pairs={{0,32},{32,0},{64,96},{96,64},{1,33},{33,1},{65,97},{97,65},{2,34}... | collective-permute-start | bytes 25165832 | tf_op jit(solution)/shard_map/ppermute | solution.py:19
  424.3 13.2 %copy-start.2 = (bf16[512,4096]{1,0:T(8,128)(2,1)S(1)}, bf16[512,4096]{1,0:T(8,128)(2,1)}, u32[]{:S(2)}) copy-start(bf16[512,4096]{1,0:T(8,128)(2,1)} %reshape.47) | copy-start | bytes 12582916
  437.5 6.3 %copy-start.4 = (f32[256]{0:T(256)S(1)}, f32[256]{0:T(256)}, u32[]{:S(2)}) copy-start(f32[256]{0:T(256)} %param.18) | copy-start | bytes 3076
  437.5 6.9 %copy-start.3 = (f32[512,4096]{1,0:T(8,128)S(1)}, f32[512,4096]{1,0:T(8,128)}, u32[]{:S(2)}) copy-start(f32[512,4096]{1,0:T(8,128)} %all-reduce.2.cloned.1.call-done) | copy-start | bytes 25165828
Sparse Core Ops, SparseCore 0:
  19.2 48.5 all-gather.1
  106.8 119.5 all-reduce.1
